TPU v7x, 256 devices: a whole 4x4x8 slice. The times are simulated.
256 devices in a mesh: row: 32 (over z, y_hi, core), col: 8 (over x, y_lo).
Axes of the slice: x: 4, y: 4 (y_hi: 2, y_lo: 2; y = y_hi * 2 + y_lo), z: 8, core: 2. Of those that a mesh axis runs over, the one named last changes fastest.
Arguments:
- activations: bfloat16 [1024, 8192], P('col', 'row'), may hold values from -0.1875 to 0.1875
- out_grad: bfloat16 [1024, 32768], P('row', 'col'), may hold values from -6 to 6
- weight: bfloat16 [8192, 32768], P('row', 'col'), may hold values from -0.03125 to 0.03125
Outputs:
- input_grad: bfloat16 [1024, 8192], P('col', 'row')
- weight_grad: bfloat16 [8192, 32768], P('row', 'col')
- left_stats: float32 [32, 8, 1, 1024, 1024], P('row', 'col')
- right_stats: float32 [32, 8, 1, 1024, 1024], P('row', 'col')
All inputs are finite; a program needn't handle non-finite values.
Results may differ from a plain program's by a relative error of at most 0.0034.
Values may be sent and summed in bfloat16 or wider, within the bound.
A program may use at most 64 MiB of HBM per device.

v0:
```python
import jax
import jax.numpy as jnp
from jax import lax
from jax.sharding import PartitionSpec as P

BLK = 1024


def from_partner(array, axis, distance):
    return lax.ppermute(array, axis, [(i, i ^ 1 << distance) for i in range(lax.axis_size(axis))])


def xor_permute(slots, position, nbits):
    size = slots.shape[0]
    shaped = slots.reshape((2,) * nbits + slots.shape[1:])
    for bit_index in range(nbits):
        flag = (position >> bit_index) % 2 == 1
        axis_number = nbits - 1 - bit_index
        shaped = jnp.where(flag, jnp.flip(shaped, axis_number), shaped)
    return shaped.reshape((size,) + slots.shape[1:])


def trade_halves(slots, bit_index):
    size = slots.shape[0]
    shaped = slots.reshape((size >> bit_index + 1, 2, 1 << bit_index) + slots.shape[1:])
    incoming = from_partner(shaped[:, 1], "row", bit_index)
    return jnp.stack([shaped[:, 0], incoming], axis=1).reshape(slots.shape)


def on_device(activations, out_grad, weight):
    rows_dev = weight.shape[0]
    cols_dev = weight.shape[1]
    full_acts = lax.all_gather(activations, "col", axis=0, tiled=True)
    panel = lax.all_gather(out_grad, "row", axis=0, tiled=True)
    grad_sum = lax.dot_general(
        full_acts, panel, (((0,), (0,)), ((), ())), preferred_element_type=jnp.float32
    )
    product = lax.dot_general(
        panel, weight, (((1,), (1,)), ((), ())), preferred_element_type=jnp.float32
    )
    input_grad = lax.psum_scatter(product, "col", scatter_dimension=0, tiled=True).astype(
        jnp.bfloat16
    )
    weight_grad = grad_sum.astype(jnp.bfloat16)
    group_size = BLK // rows_dev
    nbits = group_size.bit_length() - 1
    per_device = cols_dev // BLK // group_size
    position = lax.axis_index("row") % group_size
    slots = weight_grad.reshape(rows_dev, group_size, per_device * BLK).transpose(1, 0, 2)
    slots = xor_permute(slots, position, nbits)
    bit_list = list(range(nbits))
    for bit_index in bit_list:
        slots = trade_halves(slots, bit_index)
    ordered = xor_permute(slots, position, nbits)
    block_rows = ordered.reshape(BLK, per_device, BLK).transpose(1, 0, 2)
    left_stats = jnp.einsum(
        "pik,pjk->pij", block_rows, block_rows, preferred_element_type=jnp.float32
    ) * (1.0 / BLK)
    right_stats = jnp.einsum(
        "pki,pkj->pij", block_rows, block_rows, preferred_element_type=jnp.float32
    ) * (1.0 / BLK)
    left_stats = left_stats.reshape(1, 1, per_device, BLK, BLK)
    right_stats = right_stats.reshape(1, 1, per_device, BLK, BLK)
    return (input_grad, weight_grad, left_stats, right_stats)


def solution(mesh):
    placed = (P("col", "row"), P("row", "col"), P("row", "col"))
    return jax.shard_map(
        on_device,
        mesh=mesh,
        in_specs=placed,
        out_specs=(
            P("col", "row"),
            P("row", "col"),
            P("row", "col", None, None, None),
            P("row", "col", None, None, None),
        ),
        check_vma=False,
    )
```

profile of v0, /device:TPU:1, one launch (start us, length us, event | category | flops | bytes accessed | tf_op | source)
XLA Modules:
  0.0 198.0 jit_solution(17036838684425333287)
XLA Ops:
  7.2 0.7 all-gather.2.cloned.1.call-update
  7.9 0.0 reduce-scatter.2.cloned.1.call-start
  8.0 24.9 %all_gather.7 = bf16[1024,256]{1,0:T(8,128)(2,1)S(1)} all-gather(bf16[128,256]{1,0:T(8,128)(2,1)} %param.3), channel_id=1, replica_groups=mesh['row'=32,'col'=8] {'col'}, dimensions={0}, use_global_device_ids=true | all-gather | bytes 589824 | tf_op jit(solution)/shard_map/all_gather | solution.py:33
  32.9 84.3 %all-gather.2.cloned.1.call-done = bf16[1024,4096]{1,0:T(8,128)(2,1)} async-done(((bf16[32,4096]{1,0:T(8,128)(2,1)}), bf16[1024,4096]{1,0:T(8,128)(2,1)}) %all-gather.2.cloned.1.call-update) | async-done | bytes 8388624 | tf_op jit(solution)/shard_map/all_gather | solution.py:34
  117.3 5.8 %convolution_convert_fusion = bf16[256,4096]{1,0:T(8,128)(2,1)S(1)} fusion(bf16[1024,256]{1,0:T(8,128)(2,1)S(1)} %all_gather.7, bf16[1024,4096]{1,0:T(8,128)(2,1)} %all-gather.2.cloned.1.call-done), kind=kOutput, calls=%fused_computation | convolution fusion | flops 2148532224 | bytes 11010048 | tf_op jit(solution)/shard_map/dot_general | solution.py:35
  123.0 0.2 copy.21
  123.2 1.1 copy-done.1
  124.3 0.6 reverse_select_fusion.3
  124.9 0.6 fusion.1
  125.5 1.1 slice_bitcast_fusion.3
  126.7 0.3 collective-permute-start
  126.9 0.8 slice-done.1
  127.8 3.3 %fusion.2 = f32[1024,256]{1,0:T(8,128)} fusion(bf16[1024,4096]{1,0:T(8,128)(2,1)S(1)} %bitcast.43, bf16[256,4096]{1,0:T(8,128)(2,1)S(1)} %copy-done), kind=kOutput, calls=%fused_computation.16 | convolution fusion | flops 2147483648 | bytes 11534336 | tf_op jit(solution)/shard_map/dot_general | solution.py:38
  131.1 1.4 maximum_bitcast_fusion
  132.6 1.1 slice_bitcast_fusion.1
  133.7 0.2 collective-permute-start.1
  133.9 37.7 %reduce-scatter.2.cloned.1.call-done = f32[128,256]{1,0:T(8,128)} async-done(((f32[1024,256]{1,0:T(8,128)}), f32[128,256]{1,0:T(8,128)}) %reduce-scatter.2.cloned.1.call-update) | async-done | bytes 131088 | tf_op jit(solution)/shard_map/reduce_scatter | solution.py:41
  171.7 1.5 convert_element_type.6
  173.2 6.5 %collective-permute-done.1 = bf16[1,2,256,1024]{3,2,1,0:T(8,128)(2,1)} collective-permute-done((bf16[1,2,256,1024]{3,2,1,0:T(8,128)(2,1)}, bf16[1,2,256,1024]{3,2,1,0:T(8,128)(2,1)}, u32[]{:S(2)}, u32[]{:S(2)}) %collective-permute-start.1) | collective-permute-done | bytes 1048608 | tf_op jit(solution)/shard_map/ppermute | solution.py:10
  179.7 1.4 maximum_bitcast_fusion.1
  181.1 0.6 reverse_select_fusion.1
  181.7 0.6 reverse_select_fusion
  182.3 4.4 %fusion = f32[1,1,1,1024,1024]{4,3,2,1,0:T(8,128)} fusion(bf16[2,2,256,1024]{3,2,1,0:T(8,128)(2,1)S(1)} %reverse_select_fusion), kind=kOutput, calls=%fused_computation.2 | convolution fusion | flops 2148532224 | bytes 6291456 | tf_op jit(solution)/shard_map/pki,pkj->pij/dot_general | solution.py:59
  186.7 4.4 %multiply_bitcast_fusion = f32[1,1,1,1024,1024]{4,3,2,1,0:T(8,128)} fusion(bf16[1024,1024]{1,0:T(8,128)(2,1)S(1)} %bitcast.46), kind=kOutput, calls=%fused_computation.3 | convolution fusion | flops 2148532224 | bytes 6291456 | tf_op jit(solution)/shard_map/pik,pjk->pij/dot_general | solution.py:56
  (10 shorter events, 0.1 us)
Async XLA Ops:
  7.2 119.8 %copy-start = (bf16[256,4096]{1,0:T(8,128)(2,1)S(1)}, bf16[256,4096]{1,0:T(8,128)(2,1)}, u32[]{:S(2)}) copy-start(bf16[256,4096]{1,0:T(8,128)(2,1)} %param.5) | copy-start | bytes 6291460
  7.2 110.1 %all-gather.2.cloned.1.call-start = ((), (), s32[]{:S(2)}) async-start(), calls=%async_computation.1 | async-start | bytes 8650752 | tf_op jit(solution)/shard_map/all_gather | solution.py:34
  7.9 163.8 %reduce-scatter.2.cloned.1.call-start = ((), (), s32[]{:S(2)}) async-start(), calls=%async_computation.2 | async-start | bytes 1179648 | tf_op jit(solution)/shard_map/reduce_scatter | solution.py:41
  123.0 1.3 copy-start.1
  123.0 3.9 %slice-start = ((s8[8388608]{0:T(1024)(128)(4,1)}), s8[4194304]{0:T(1024)(128)(4,1)S(1)}, s32[]{:S(2)}) async-start(s8[8388608]{0:T(1024)(128)(4,1)} %bitcast.42), calls=%async_computation.3 | async-start | bytes 8388608
  124.3 3.4 %slice-start.1 = ((s8[8388608]{0:T(1024)(128)(4,1)}), s8[4194304]{0:T(1024)(128)(4,1)S(1)}, s32[]{:S(2)}) async-start(s8[8388608]{0:T(1024)(128)(4,1)} %bitcast.42), calls=%async_computation.4 | async-start | bytes 8388608
  126.7 4.4 %collective-permute-start = (bf16[2,1,256,1024]{3,2,0,1:T(8,128)(2,1)}, bf16[2,1,256,1024]{3,2,0,1:T(8,128)(2,1)}, u32[]{:S(2)}, u32[]{:S(2)}) collective-permute-start(bf16[2,1,256,1024]{3,2,0,1:T(8,128)(2,1)} %get-tuple-element.7), channel_id=1, source_target_pairs={{0,8},{8,0},{16,24},{24,16},{32,40},{40,32},{48,56},{56,48},{64,72... | collective-permute-start | bytes 3145736 | tf_op jit(solution)/shard_map/ppermute | solution.py:10
  133.7 46.0 %collective-permute-start.1 = (bf16[1,2,256,1024]{3,2,1,0:T(8,128)(2,1)}, bf16[1,2,256,1024]{3,2,1,0:T(8,128)(2,1)}, u32[]{:S(2)}, u32[]{:S(2)}) collective-permute-start(bf16[1,2,256,1024]{3,2,1,0:T(8,128)(2,1)} %get-tuple-element.5), channel_id=1, source_target_pairs={{0,16},{8,24},{16,0},{24,8},{32,48},{40,56},{48,32},{56,40},{64,80... | collective-permute-start | bytes 3145736 | tf_op jit(solution)/shard_map/ppermute | solution.py:10
Sparse Core Ops, SparseCore 0:
  10.8 106.4 all-gather.1
  131.3 40.3 reduce-scatter.1
where the time goes:
time: 198 us
  waiting for transfers between devices  129 us (65%)
  blocking collectives  24.9 us (13%)
  matrix products  17.9 us (9%)
  between operations  14.2 us (7%)
  other arithmetic  6.72 us (3%)
  local copies, waits for them, and re-layouts  4.42 us (2%)
    all_gather x1, waiting for transfers between devices, on_device(): panel = lax.all_gather(out_grad, 'row', axis=0, tiled=True)  84.3 us
    reduce_scatter x1, waiting for transfers between devices, on_device(): lax.psum_scatter(product, 'col', scatter_dimension=0, tiled=True)  37.7 us
    all_gather x1, blocking collectives, on_device(): full_acts = lax.all_gather(activations, 'col', axis=0, tiled=True)  24.9 us
    ppermute x2, waiting for transfers between devices, from_partner(): lax.ppermute(array, axis, [(i, i ^ 1 << distance) for i in range(lax.axis...  6.47 us
    dot_general x1, matrix products, on_device(): lax.dot_general(full_acts, panel, (((0,), (0,)), ((), ())), preferred_ele...  5.75 us
    dot_general x1, matrix products, on_device(): jnp.einsum('pki,pkj->pij', block_rows, block_rows, preferred_element_type...  4.43 us
    dot_general x1, matrix products, on_device(): jnp.einsum('pik,pjk->pij', block_rows, block_rows, preferred_element_type...  4.39 us
    unnamed x10, local copies, waits for them, and re-layouts  4.25 us
  transfers between devices with their start and end apart: 4, of which 3 were waited for; matrix products, arithmetic and copies ran while one was open for 4% of the time, Pallas kernels for 0%

commit v1 on v0

v1 whole, which is shorter than its diff:
```python
import functools

import jax
import jax.numpy as jnp
from jax import lax
from jax.experimental import pallas as pl
from jax.experimental.pallas import tpu as pltpu
from jax.sharding import PartitionSpec as P

MESH = pl.DeviceIdType.MESH
F32 = jnp.float32
BF16 = jnp.bfloat16


def gather_kernel(
    acts_ref, og_ref, w_ref,
    ig_ref, wg_ref, g_ref,
    panel, w_v, acts, wacc, gacc, stage, inbox,
    local_sem, zsend, zrecv, ysend, yrecv, msend, mrecv,
    aysend, ayrecv, asend, arecv, amsend, amrecv, rsend, rrecv,
):
    row, col = lax.axis_index("row"), lax.axis_index("col")
    z, line, core = row // 4, lax.rem(row // 2, 2), lax.rem(row, 2)
    member = 2 * line + core
    half = og_ref.shape[1] // 2
    quarter = og_ref.shape[1] // 4
    up = (lax.rem(z + 1, 8) * 4 + member, col)
    down = (lax.rem(z + 7, 8) * 4 + member, col)
    across = (z * 4 + 2 * (1 - line) + core, col)
    mate = (z * 4 + 2 * line + 1 - core, col)

    def peer(step):
        return (row, lax.rem(col + step, 8))

    def remote(src, dst, send, recv, device):
        return pltpu.make_async_remote_copy(
            src_ref=src, dst_ref=dst, send_sem=send, recv_sem=recv,
            device_id=device, device_id_type=MESH,
        )

    barrier = pltpu.get_barrier_semaphore()
    for device in [up, down, across, mate] + [peer(step) for step in range(1, 8)]:
        pl.semaphore_signal(barrier, inc=1, device_id=device, device_id_type=MESH)
    pl.semaphore_wait(barrier, 11)

    def plane(distance, way):
        return lax.rem(z + 8 - distance if way == 0 else z + distance, 8)

    def block(where, of_partner, other_core=False):
        which = 1 - line if of_partner else line
        return where * 4 + 2 * which + (1 - core if other_core else core)

    def zref(ref, step, way):
        if step < 4:
            return ref
        return ref.at[:, pl.ds(way * half, half)]

    def zcopy(of_partner, step, way):
        index = block(plane(step - 1, way), of_partner)
        source = og_ref if step == 1 and not of_partner else panel.at[index]
        slot = (way, int(of_partner), step - 1)
        return remote(
            zref(source, step, way), zref(panel.at[index], step, way),
            zsend.at[slot], zrecv.at[slot], up if way == 0 else down,
        )

    def zarrive(of_partner, step, way):
        index = block(plane(step, way), of_partner)
        here = zref(panel.at[index], step, way)
        slot = (way, int(of_partner), step - 1)
        remote(here, here, zsend.at[slot], zrecv.at[slot], up if way == 0 else down).wait_recv()

    def to_mate(where, of_partner, source=None):
        index = block(where, of_partner)
        slot = where * 2 + (1 - line if of_partner else line)
        return remote(
            panel.at[index] if source is None else source, panel.at[index],
            msend.at[slot], mrecv.at[slot], mate,
        )

    def from_mate(where, of_partner):
        index = block(where, of_partner, True)
        slot = where * 2 + (1 - line if of_partner else line)
        here = panel.at[index]
        remote(here, here, msend.at[slot], mrecv.at[slot], mate).wait_recv()

    for way in range(2):
        zcopy(False, 1, way).start()
    to_across = remote(og_ref, panel.at[row], ysend, yrecv, across)
    to_across.start()
    to_mate(z, False, og_ref).start()
    own_copy = pltpu.make_async_copy(og_ref, panel.at[row], local_sem.at[0])
    own_copy.start()
    w_copy = pltpu.make_async_copy(w_ref, w_v, local_sem.at[1])
    w_copy.start()

    acts[core, col, line] = acts_ref[...].astype(F32).T.astype(BF16)
    mine = acts.at[core, col, line]
    act_across = remote(mine, mine, aysend, ayrecv, across)
    act_across.start()
    other = acts.at[core, col, 1 - line]
    remote(other, other, aysend, ayrecv, across).wait_recv()
    pair = acts.at[core, col]

    def act_send(step):
        return remote(pair, pair, asend.at[step], arecv.at[col], peer(step))

    def act_mate(where):
        ref = acts.at[core, where]
        return remote(ref, ref, amsend.at[where], amrecv.at[where], mate)

    for step in range(1, 8):
        act_send(step).start()
    act_mate(col).start()

    def forward(of_partner, step):
        for way in range(2):
            zarrive(of_partner, step, way)
            if step < 4:
                zcopy(of_partner, step + 1, way).start()
                to_mate(plane(step, way), of_partner).start()
        if step == 4:
            to_mate(plane(4, 0), of_partner).start()

    def chunk(where, columns):
        return panel[pl.ds(where * 4, 4), :, columns].reshape(128, columns.size)

    def input_grad(planes):
        tokens = 128 * len(planes)

        def add(k, total):
            columns = pl.ds(pl.multiple_of(k * quarter, quarter), quarter)
            lhs = jnp.concatenate([chunk(where, columns) for where in planes], axis=0)
            return total + lax.dot_general(
                lhs, w_v[:, columns], (((1,), (1,)), ((), ())), preferred_element_type=F32
            )

        total = lax.fori_loop(0, 4, add, jnp.zeros((tokens, w_v.shape[0]), F32))
        for i, where in enumerate(planes):
            stage[where] = total[i * 128:(i + 1) * 128]

            @pl.when(where != col)
            def _():
                sum_send(where).start()

    def sum_send(where):
        return remote(stage.at[where], inbox.at[col], rsend.at[where], rrecv.at[col], (row, where))

    def weight_grad(planes, first=False, last=False):
        def lhs_of(of_core, of_line):
            return jnp.concatenate([acts[of_core, where, of_line] for where in planes], axis=1)

        def rhs_of(columns):
            return jnp.concatenate([chunk(where, columns) for where in planes], axis=0)

        def own(t, carry):
            columns = pl.ds(pl.multiple_of(t * 512, 512), 512)
            out = jnp.dot(lhs_of(core, line), rhs_of(columns), preferred_element_type=F32)
            if not first:
                out = out + wacc[:, columns]
            if last:
                wg_ref[:, columns] = out.astype(BF16)
            else:
                wacc[:, columns] = out
            return carry

        lax.fori_loop(0, 8, own, 0)

        def others(t, carry):
            which = lax.rem(member + 1 + t // 2, 4)
            columns = pl.ds(pl.multiple_of(member * quarter + lax.rem(t, 2) * 512, 512), 512)
            place = pl.ds(pl.multiple_of(lax.rem(t, 2) * 512, 512), 512)
            out = jnp.dot(
                lhs_of(lax.rem(which, 2), which // 2), rhs_of(columns), preferred_element_type=F32
            )
            if not first:
                out = out + gacc[which, :, place]
            if last:
                g_ref[which, :, place] = out.astype(BF16)
            else:
                gacc[which, :, place] = out
            return carry

        lax.fori_loop(0, 6, others, 0)

    def both(step):
        return [plane(step, 0), plane(step, 1)]

    def from_mate_all(planes):
        for where in planes:
            from_mate(where, False)
            from_mate(where, True)

    forward(False, 1)
    here = panel.at[block(z, True)]
    remote(here, here, ysend, yrecv, across).wait_recv()
    for way in range(2):
        zcopy(True, 1, way).start()
    to_mate(z, True).start()
    own_copy.wait()
    w_copy.wait()
    from_mate_all([z])
    input_grad([z])

    def act_forward(step, carry):
        where = lax.rem(col + step, 8)
        ref = acts.at[core, where]
        remote(ref, ref, asend.at[step], arecv.at[where], mate).wait_recv()
        act_mate(where).start()
        return carry

    forward(False, 2)
    lax.fori_loop(1, 8, act_forward, 0)
    forward(True, 1)
    from_mate_all(both(1))
    input_grad(both(1))

    def act_from_mate(where, carry):
        ref = acts.at[1 - core, where]
        remote(ref, ref, amsend.at[where], amrecv.at[where], mate).wait_recv()
        return carry

    lax.fori_loop(0, 8, act_from_mate, 0)
    forward(False, 3)
    weight_grad(both(1), first=True)
    forward(True, 2)
    from_mate_all(both(2))
    input_grad(both(2))
    forward(False, 4)
    weight_grad(both(2))
    forward(True, 3)
    from_mate_all(both(3))
    input_grad(both(3))
    weight_grad(both(3))
    forward(True, 4)
    from_mate_all([plane(4, 0)])
    input_grad([plane(4, 0)])
    weight_grad([z, plane(4, 0)], last=True)
    g_ref[member] = wg_ref[:, pl.ds(pl.multiple_of(member * quarter, quarter), quarter)]

    def take(step, total):
        where = lax.rem(col + step, 8)
        ref = inbox.at[where]
        remote(ref, ref, rsend.at[where], rrecv.at[where], (row, where)).wait_recv()
        return total + inbox[where]

    ig_ref[...] = lax.fori_loop(1, 8, take, stage[col]).astype(BF16)

    for way in range(2):
        for of_partner in (False, True):
            for step in range(1, 5):
                zcopy(of_partner, step, way).wait_send()
    to_across.wait_send()
    act_across.wait_send()

    def drain(where, carry):
        for of_line in range(2):
            index = where * 4 + 2 * of_line + core
            slot = where * 2 + of_line
            ref = panel.at[index]
            remote(ref, ref, msend.at[slot], mrecv.at[slot], mate).wait_send()
        act_mate(where).wait_send()
        return carry

    lax.fori_loop(0, 8, drain, 0)

    def drain_peers(step, carry):
        act_send(step).wait_send()
        sum_send(lax.rem(col + step, 8)).wait_send()
        return carry

    lax.fori_loop(1, 8, drain_peers, 0)


def gram_kernel(g_ref, wg_in, left_ref, right_ref, wg_out):
    i = pl.program_id(0)
    size = left_ref.shape[0]
    rows = pl.ds(pl.multiple_of(i * size, size), size)
    wg_out[...] = wg_in[...]
    scale = 1.0 / g_ref.shape[0]
    left_ref[...] = scale * lax.dot_general(
        g_ref[rows, :], g_ref[...], (((1,), (1,)), ((), ())), preferred_element_type=F32
    )
    right_ref[...] = scale * lax.dot_general(
        g_ref[:, rows], g_ref[...], (((0,), (0,)), ((), ())), preferred_element_type=F32
    )


def on_device(activations, out_grad, weight):
    tokens, feats = activations.shape
    rows, cols = weight.shape
    vmem = pl.BlockSpec(memory_space=pltpu.VMEM)
    anywhere = pl.BlockSpec(memory_space=pl.ANY)
    dma = pltpu.SemaphoreType.DMA
    quarter = cols // 4
    input_grad, weight_grad, blocks = pl.pallas_call(
        gather_kernel,
        out_shape=(
            jax.ShapeDtypeStruct((tokens, feats), BF16),
            jax.ShapeDtypeStruct((rows, cols), BF16),
            jax.ShapeDtypeStruct((4, rows, quarter), BF16),
        ),
        in_specs=[vmem, anywhere, anywhere],
        out_specs=(vmem, vmem, vmem),
        scratch_shapes=[
            pltpu.VMEM((32, out_grad.shape[0], cols), BF16),
            pltpu.VMEM((rows, cols), BF16),
            pltpu.VMEM((2, 8, 2, feats, tokens), BF16),
            pltpu.VMEM((rows, cols), F32),
            pltpu.VMEM((4, rows, quarter), F32),
            pltpu.VMEM((8, tokens, feats), F32),
            pltpu.VMEM((8, tokens, feats), F32),
            dma((2,)),
            dma((2, 2, 4)), dma((2, 2, 4)), dma, dma, dma((16,)), dma((16,)),
            dma, dma, dma((8,)), dma((8,)), dma((8,)), dma((8,)), dma((8,)), dma((8,)),
        ],
        compiler_params=pltpu.CompilerParams(
            collective_id=0, has_side_effects=True, vmem_limit_bytes=44 * 2**20
        ),
        name="gather_and_grads",
    )(activations, out_grad, weight)

    size = 4 * rows
    step = size // 4
    left, right, weight_grad = pl.pallas_call(
        gram_kernel,
        grid=(4,),
        out_shape=(
            jax.ShapeDtypeStruct((size, quarter), F32),
            jax.ShapeDtypeStruct((quarter, quarter), F32),
            jax.ShapeDtypeStruct((rows, cols), BF16),
        ),
        in_specs=[
            pl.BlockSpec((size, quarter), lambda i: (0, 0)),
            pl.BlockSpec((rows // 4, cols), lambda i: (i, 0)),
        ],
        out_specs=(
            pl.BlockSpec((step, quarter), lambda i: (i, 0)),
            pl.BlockSpec((step, quarter), lambda i: (i, 0)),
            pl.BlockSpec((rows // 4, cols), lambda i: (i, 0)),
        ),
        compiler_params=pltpu.CompilerParams(vmem_limit_bytes=32 * 2**20),
        name="grams",
    )(blocks.reshape(size, quarter), weight_grad)
    return (
        input_grad,
        weight_grad,
        left.reshape(1, 1, 1, size, quarter),
        right.reshape(1, 1, 1, quarter, quarter),
    )


def solution(mesh):
    return jax.shard_map(
        on_device,
        mesh=mesh,
        in_specs=(P("col", "row"), P("row", "col"), P("row", "col")),
        out_specs=(
            P("col", "row"),
            P("row", "col"),
            P("row", "col", None, None, None),
            P("row", "col", None, None, None),
        ),
        check_vma=False,
    )
```

time: 198 us -> 82.4 us (0.42)
  the two profiles are of different devices: /device:TPU:1 before, /device:TPU:21 now
where the time goes in v1:
time: 82.4 us; the launch traced here: 82.3 us
  Pallas kernels  77.6 us (94%)
  local copies, waits for them, and re-layouts  4 us (5%)
    pallas_call x1, Pallas kernels, on_device(): pl.pallas_call(gather_kernel, out_shape=(jax.ShapeDtypeStruct((tokens, fe...  71.3 us
    pallas_call x1, Pallas kernels, on_device(): pl.pallas_call(gram_kernel, grid=(4,), out_shape=(jax.ShapeDtypeStruct((s...  6.34 us
    unnamed x7, local copies, waits for them, and re-layouts  4 us

profile of v1, /device:TPU:21, one launch (start us, length us, event | category | flops | bytes accessed | tf_op | source)
XLA Modules:
  0.0 82.3 jit_solution(14293066520485515658)
XLA Ops:
  0.6 0.0 copy-start
  0.6 1.6 %copy-done = bf16[256,4096]{1,0:T(8,128)(2,1)S(1)} copy-done((bf16[256,4096]{1,0:T(8,128)(2,1)S(1)}, bf16[256,4096]{1,0:T(8,128)(2,1)}, u32[]{:S(2)}) %copy-start) | copy-done | bytes 2097176
  2.2 0.0 copy-start.1
  2.2 0.9 %copy-done.1 = bf16[32,4096]{1,0:T(8,128)(2,1)S(1)} copy-done((bf16[32,4096]{1,0:T(8,128)(2,1)S(1)}, bf16[32,4096]{1,0:T(8,128)(2,1)}, u32[]{:S(2)}) %copy-start.1) | copy-done | bytes 262168
  3.2 0.0 copy-start.2
  3.2 0.8 %copy-done.2 = bf16[128,256]{1,0:T(8,128)(2,1)S(1)} copy-done((bf16[128,256]{1,0:T(8,128)(2,1)S(1)}, bf16[128,256]{1,0:T(8,128)(2,1)}, u32[]{:S(2)}) %copy-start.2) | copy-done | bytes 65560
  4.0 71.3 %gather_and_grads.1 = (bf16[128,256]{1,0:T(8,128)(2,1)S(1)}, bf16[256,4096]{1,0:T(8,128)(2,1)S(1)}, bf16[4,256,1024]{2,1,0:T(8,128)(2,1)S(1)}) custom-call(bf16[128,256]{1,0:T(8,128)(2,1)S(1)} %copy-done.2, bf16[32,4096]{1,0:T(8,128)(2,1)S(1)} %copy-done.1, bf16[256,4096]{1,0:T(8,128)(2,1)S(1)} %copy-done), custom_call_target="tpu_custom_call" | custom-call | tf_op jit(solution)/shard_map/gather_and_grads/pallas_call | solution.py:296
  75.3 6.3 %grams.1 = (f32[1024,1024]{1,0:T(8,128)}, f32[1024,1024]{1,0:T(8,128)}, bf16[256,4096]{1,0:T(8,128)(2,1)}) custom-call(bf16[1024,1024]{1,0:T(8,128)(2,1)S(1)} %bitcast.3, bf16[256,4096]{1,0:T(8,128)(2,1)S(1)} %get-tuple-element.12.wg_in), custom_call_target="tpu_custom_call" | custom-call | tf_op jit(solution)/shard_map/grams/pallas_call | solution.py:325
  81.6 0.6 copy.8
Async XLA Ops:
  0.6 1.6 %copy-start = (bf16[256,4096]{1,0:T(8,128)(2,1)S(1)}, bf16[256,4096]{1,0:T(8,128)(2,1)}, u32[]{:S(2)}) copy-start(bf16[256,4096]{1,0:T(8,128)(2,1)} %w_ref.1) | copy-start | bytes 6291460
  2.2 0.9 %copy-start.1 = (bf16[32,4096]{1,0:T(8,128)(2,1)S(1)}, bf16[32,4096]{1,0:T(8,128)(2,1)}, u32[]{:S(2)}) copy-start(bf16[32,4096]{1,0:T(8,128)(2,1)} %og_ref.1) | copy-start | bytes 786436
  3.2 0.8 %copy-start.2 = (bf16[128,256]{1,0:T(8,128)(2,1)S(1)}, bf16[128,256]{1,0:T(8,128)(2,1)}, u32[]{:S(2)}) copy-start(bf16[128,256]{1,0:T(8,128)(2,1)} %acts_ref.1) | copy-start | bytes 196612

commit v2 on v1

v2 whole, which is shorter than its diff:
```python
import functools

import jax
import jax.numpy as jnp
from jax import lax
from jax.experimental import pallas as pl
from jax.experimental.pallas import tpu as pltpu
from jax.sharding import PartitionSpec as P

MESH = pl.DeviceIdType.MESH
F32 = jnp.float32
BF16 = jnp.bfloat16


def gather_kernel(
    acts_ref, og_ref, w_ref,
    ig_ref, wg_ref, g_ref,
    panel, w_v, acts_v, acts, wacc, gacc, wide, wide_in, slim, slim_in,
    local_sem, zsend, zrecv, ysend, yrecv, msend, mrecv,
    aysend, ayrecv, axsend, axrecv, amsend, amrecv, rsend, rrecv,
):
    row, col = lax.axis_index("row"), lax.axis_index("col")
    z, line, core = row // 4, lax.rem(row // 2, 2), lax.rem(row, 2)
    x, side = col // 2, lax.rem(col, 2)
    member = 2 * line + core
    half = og_ref.shape[1] // 2
    quarter = og_ref.shape[1] // 4
    up = (lax.rem(z + 1, 8) * 4 + member, col)
    down = (lax.rem(z + 7, 8) * 4 + member, col)
    far_row = z * 4 + 2 * (1 - line) + core
    across = (far_row, col)
    mate = (z * 4 + 2 * line + 1 - core, col)
    beside = (row, x * 2 + 1 - side)
    corner = (far_row, x * 2 + 1 - side)

    def x_peer(step, other=False):
        return (row, lax.rem(x + step, 4) * 2 + (1 - side if other else side))

    def remote(src, dst, send, recv, device):
        return pltpu.make_async_remote_copy(
            src_ref=src, dst_ref=dst, send_sem=send, recv_sem=recv,
            device_id=device, device_id_type=MESH,
        )

    act_copy = pltpu.make_async_copy(acts_ref, acts_v, local_sem.at[2])
    act_copy.start()
    barrier = pltpu.get_barrier_semaphore()
    peers = [up, down, across, mate, beside, corner]
    peers += [x_peer(step) for step in range(1, 4)] + [x_peer(step, True) for step in range(1, 4)]
    for device in peers:
        pl.semaphore_signal(barrier, inc=1, device_id=device, device_id_type=MESH)
    pl.semaphore_wait(barrier, len(peers))

    def plane(distance, way):
        return lax.rem(z + 8 - distance if way == 0 else z + distance, 8)

    def part(ref, which):
        return ref.at[:, pl.ds(which * half, half)]

    def block(where, of_partner):
        return panel.at[where * 4 + 2 * (1 - line if of_partner else line) + core]

    def zcopy(of_partner, step, way, which):
        slot = (way, int(of_partner), step - 1, which)
        target = block(plane(step - 1, way), of_partner)
        source = og_ref if step == 1 else target
        return remote(
            part(source, which), part(target, which),
            zsend.at[slot], zrecv.at[slot], up if way == 0 else down,
        )

    def zwait(of_partner, step, way, which):
        slot = (way, int(of_partner), step - 1, which)
        here = part(block(plane(step, way), of_partner), which)
        remote(here, here, zsend.at[slot], zrecv.at[slot], up if way == 0 else down).wait_recv()

    def yplane(slot):
        return (z, plane(1, 0), plane(1, 1), plane(4, 0))[slot]

    def ycopy(slot, which):
        target = block(yplane(slot), False)
        source = og_ref if slot == 0 else target
        return remote(
            part(source, which), part(target, which),
            ysend.at[slot, which], yrecv.at[slot, which], across,
        )

    def ywait(slot, which):
        here = part(block(yplane(slot), True), which)
        remote(here, here, ysend.at[slot, which], yrecv.at[slot, which], across).wait_recv()

    def mcopy(where, of_line, which, of_core, source=None):
        target = part(panel.at[where * 4 + 2 * of_line + of_core], which)
        slot = (where * 2 + of_line, which)
        return remote(
            target if source is None else part(source, which), target,
            msend.at[slot], mrecv.at[slot], mate,
        )

    def hand(where, of_partner, which, source=None):
        mcopy(where, 1 - line if of_partner else line, which, core, source).start()

    def from_mate(where, of_partner):
        for which in range(2):
            mcopy(where, 1 - line if of_partner else line, which, 1 - core).wait_recv()

    for which in range(2):
        for way in range(2):
            zcopy(False, 1, way, which).start()
        ycopy(0, which).start()
    own_copy = pltpu.make_async_copy(og_ref, panel.at[row], local_sem.at[0])
    own_copy.start()
    w_copy = pltpu.make_async_copy(w_ref, w_v, local_sem.at[1])
    w_copy.start()
    for which in range(2):
        hand(z, False, which, og_ref)

    act_copy.wait()
    acts[core, x, 2 * side + line] = acts_v[...].astype(F32).T.astype(BF16)

    def act_y(slot):
        mine = acts.at[core, x, 2 * side + line]
        return remote(mine, mine, aysend.at[slot], ayrecv.at[slot], (across, beside, corner)[slot])

    def act_y_wait(slot):
        place = (2 * side + 1 - line, 2 * (1 - side) + line, 2 * (1 - side) + 1 - line)[slot]
        here = acts.at[core, x, place]
        remote(here, here, aysend.at[slot], ayrecv.at[slot], across).wait_recv()

    def act_x(step):
        mine = acts.at[core, x]
        return remote(mine, mine, axsend.at[step], axrecv.at[step], x_peer(step))

    def act_x_wait(step):
        here = acts.at[core, lax.rem(x + 4 - step, 4)]
        remote(here, here, axsend.at[step], axrecv.at[step], x_peer(step)).wait_recv()

    def act_m(where, of_core):
        ref = acts.at[of_core, where]
        return remote(ref, ref, amsend.at[where], amrecv.at[where], mate)

    for slot in range(3):
        act_y(slot).start()

    def chunk(where, of_line, columns):
        return panel[pl.ds(where * 4 + 2 * of_line, 2), :, columns].reshape(64, columns.size)

    def wide_send(where, of_line):
        return remote(
            wide.at[where, of_line], wide_in.at[col, of_line],
            rsend.at[where, of_line], rrecv.at[col, of_line], (row, where),
        )

    def slim_send(where, of_line):
        return remote(
            slim.at[where, of_line], slim_in.at[col, of_line],
            rsend.at[where, of_line], rrecv.at[col, of_line], (row, where),
        )

    def input_grad(pieces):
        pieces = [(where, 1 - line if of_partner else line) for where, of_partner in pieces]

        def add(k, total):
            columns = pl.ds(pl.multiple_of(k * quarter, quarter), quarter)
            lhs = jnp.concatenate([chunk(*piece, columns) for piece in pieces], axis=0)
            return total + lax.dot_general(
                lhs, w_v[:, columns], (((1,), (1,)), ((), ())), preferred_element_type=F32
            )

        total = lax.fori_loop(0, 4, add, jnp.zeros((64 * len(pieces), w_v.shape[0]), F32))
        for i, (where, of_line) in enumerate(pieces):
            value = total[i * 64:(i + 1) * 64]
            same = lax.rem(where, 2) == side

            @pl.when(same)
            def _():
                wide[where, of_line] = value

            @pl.when(same & (where != col))
            def _():
                wide_send(where, of_line).start()

            @pl.when(jnp.logical_not(same))
            def _():
                slim[where, of_line] = value.astype(BF16)
                slim_send(where, of_line).start()

    def weight_grad(planes, first=False, last=False):
        def lhs_of(of_core, of_line):
            return jnp.concatenate(
                [acts[of_core, where // 2, 2 * lax.rem(where, 2) + of_line] for where in planes], axis=1
            )

        def rhs_of(columns):
            return jnp.concatenate(
                [panel[pl.ds(where * 4, 4), :, columns].reshape(128, columns.size) for where in planes],
                axis=0,
            )

        def own(t, carry):
            columns = pl.ds(pl.multiple_of(t * 512, 512), 512)
            out = jnp.dot(lhs_of(core, line), rhs_of(columns), preferred_element_type=F32)
            if not first:
                out = out + wacc[:, columns]
            if last:
                wg_ref[:, columns] = out.astype(BF16)
            else:
                wacc[:, columns] = out
            return carry

        lax.fori_loop(0, 8, own, 0)

        def others(t, carry):
            which = lax.rem(member + 1 + t // 2, 4)
            columns = pl.ds(pl.multiple_of(member * quarter + lax.rem(t, 2) * 512, 512), 512)
            place = pl.ds(pl.multiple_of(lax.rem(t, 2) * 512, 512), 512)
            out = jnp.dot(
                lhs_of(lax.rem(which, 2), which // 2), rhs_of(columns), preferred_element_type=F32
            )
            if not first:
                out = out + gacc[which, :, place]
            if last:
                g_ref[which, :, place] = out.astype(BF16)
            else:
                gacc[which, :, place] = out
            return carry

        lax.fori_loop(0, 6, others, 0)

    def pair(step):
        return [plane(step, 0), plane(step, 1)]

    def from_z(of_partner, step, which):
        for way in range(2):
            zwait(of_partner, step, way, which)
            if step < 3:
                zcopy(of_partner, step + 1, way, which).start()
            elif step == 3 and not of_partner and way == which:
                zcopy(False, 4, way, which).start()
            if step == 1:
                ycopy(1 + way, which).start()
            hand(plane(step, way), of_partner, which)

    def from_y_near(which):
        for way in range(2):
            ywait(1 + way, which)
            zcopy(True, 2, way, which).start()
            hand(plane(1, way), True, which)

    from_z(False, 1, 0)
    from_z(False, 1, 1)
    for which in range(2):
        ywait(0, which)
        hand(z, True, which)
    for slot in range(3):
        act_y_wait(slot)
    for step in range(1, 4):
        act_x(step).start()
    act_m(x, core).start()
    from_z(False, 2, 0)
    own_copy.wait()
    w_copy.wait()
    from_mate(z, False)
    from_z(False, 2, 1)
    from_y_near(0)
    from_mate(z, True)
    input_grad([(z, False), (z, True)])
    from_z(False, 3, 0)
    for where in pair(1):
        from_mate(where, False)
    input_grad([(where, False) for where in pair(1)])
    from_y_near(1)
    from_z(False, 3, 1)
    for step in range(1, 4):
        act_x_wait(step)
        act_m(lax.rem(x + 4 - step, 4), core).start()
    for where in pair(2):
        from_mate(where, False)
    input_grad([(where, False) for where in pair(2)])
    for way in range(2):
        zwait(False, 4, way, way)
        ycopy(3, way).start()
        hand(plane(4, 0), False, way)
    for where in pair(1):
        from_mate(where, True)
    input_grad([(where, True) for where in pair(1)])
    from_z(True, 2, 0)
    for where in pair(3):
        from_mate(where, False)
    input_grad([(where, False) for where in pair(3)])
    for where in range(4):
        act_m(where, 1 - core).wait_recv()
    from_z(True, 2, 1)
    weight_grad(pair(1), first=True)
    for which in range(2):
        ywait(3, which)
        hand(plane(4, 0), True, which)
    for where in pair(2):
        from_mate(where, True)
    input_grad([(where, True) for where in pair(2)])
    from_mate(plane(4, 0), False)
    from_mate(plane(4, 0), True)
    input_grad([(plane(4, 0), False), (plane(4, 0), True)])
    from_z(True, 3, 0)
    weight_grad(pair(2))
    weight_grad([z, plane(4, 0)])
    from_z(True, 3, 1)
    for where in pair(3):
        from_mate(where, True)
    input_grad([(where, True) for where in pair(3)])
    weight_grad(pair(3), last=True)
    g_ref[member] = wg_ref[:, pl.ds(pl.multiple_of(member * quarter, quarter), quarter)]

    for of_line in range(2):
        rows = pl.ds(of_line * 64, 64)

        def take_wide(step, total):
            where = lax.rem(x + step, 4) * 2 + side
            ref = wide_in.at[where, of_line]
            remote(ref, ref, rsend.at[where, of_line], rrecv.at[where, of_line], (row, where)).wait_recv()
            return total + wide_in[where, of_line]

        def take_slim(step, total):
            where = lax.rem(x + step, 4) * 2 + 1 - side
            ref = slim_in.at[where, of_line]
            remote(ref, ref, rsend.at[where, of_line], rrecv.at[where, of_line], (row, where)).wait_recv()
            return total + slim_in[where, of_line].astype(F32)

        total = lax.fori_loop(1, 4, take_wide, wide[col, of_line])
        ig_ref[rows, :] = lax.fori_loop(0, 4, take_slim, total).astype(BF16)

    for way in range(2):
        for which in range(2):
            for step in range(1, 4):
                zcopy(False, step, way, which).wait_send()
            for step in range(2, 4):
                zcopy(True, step, way, which).wait_send()
        zcopy(False, 4, way, way).wait_send()
    for slot in range(4):
        for which in range(2):
            ycopy(slot, which).wait_send()
    for slot in range(3):
        act_y(slot).wait_send()
        act_x(slot + 1).wait_send()

    def drain(where, carry):
        for of_line in range(2):
            for which in range(2):
                mcopy(where, of_line, which, core).wait_send()
        return carry

    lax.fori_loop(0, 8, drain, 0)
    for where in range(4):
        act_m(where, core).wait_send()

    def drain_sums(step, carry):
        for of_line in range(2):
            @pl.when(step > 0)
            def _():
                wide_send(lax.rem(x + step, 4) * 2 + side, of_line).wait_send()

            slim_send(lax.rem(x + step, 4) * 2 + 1 - side, of_line).wait_send()
        return carry

    lax.fori_loop(0, 4, drain_sums, 0)


def gram_kernel(g_ref, wg_in, left_ref, right_ref, wg_out):
    i = pl.program_id(0)
    size = left_ref.shape[0]
    rows = pl.ds(pl.multiple_of(i * size, size), size)
    wg_out[...] = wg_in[...]
    scale = 1.0 / g_ref.shape[0]
    left_ref[...] = scale * lax.dot_general(
        g_ref[rows, :], g_ref[...], (((1,), (1,)), ((), ())), preferred_element_type=F32
    )
    right_ref[...] = scale * lax.dot_general(
        g_ref[:, rows], g_ref[...], (((0,), (0,)), ((), ())), preferred_element_type=F32
    )


def on_device(activations, out_grad, weight):
    tokens, feats = activations.shape
    rows, cols = weight.shape
    vmem = pl.BlockSpec(memory_space=pltpu.VMEM)
    anywhere = pl.BlockSpec(memory_space=pltpu.HBM)
    dma = pltpu.SemaphoreType.DMA
    quarter = cols // 4
    input_grad, weight_grad, blocks = pl.pallas_call(
        gather_kernel,
        out_shape=(
            jax.ShapeDtypeStruct((tokens, feats), BF16),
            jax.ShapeDtypeStruct((rows, cols), BF16),
            jax.ShapeDtypeStruct((4, rows, quarter), BF16),
        ),
        in_specs=[anywhere, anywhere, anywhere],
        out_specs=(vmem, vmem, vmem),
        scratch_shapes=[
            pltpu.VMEM((32, out_grad.shape[0], cols), BF16),
            pltpu.VMEM((rows, cols), BF16),
            pltpu.VMEM((tokens, feats), BF16),
            pltpu.VMEM((2, 4, 4, feats, tokens), BF16),
            pltpu.VMEM((rows, cols), F32),
            pltpu.VMEM((4, rows, quarter), F32),
            pltpu.VMEM((8, 2, tokens // 2, feats), F32),
            pltpu.VMEM((8, 2, tokens // 2, feats), F32),
            pltpu.VMEM((8, 2, tokens // 2, feats), BF16),
            pltpu.VMEM((8, 2, tokens // 2, feats), BF16),
            dma((3,)),
            dma((2, 2, 4, 2)), dma((2, 2, 4, 2)), dma((4, 2)), dma((4, 2)), dma((16, 2)), dma((16, 2)),
            dma((3,)), dma((3,)), dma((4,)), dma((4,)), dma((4,)), dma((4,)), dma((8, 2)), dma((8, 2)),
        ],
        compiler_params=pltpu.CompilerParams(
            collective_id=0, has_side_effects=True, vmem_limit_bytes=44 * 2**20
        ),
        name="gather_and_grads",
    )(activations, out_grad, weight)

    size = 4 * rows
    step = size // 4
    left, right, weight_grad = pl.pallas_call(
        gram_kernel,
        grid=(4,),
        out_shape=(
            jax.ShapeDtypeStruct((size, quarter), F32),
            jax.ShapeDtypeStruct((quarter, quarter), F32),
            jax.ShapeDtypeStruct((rows, cols), BF16),
        ),
        in_specs=[
            pl.BlockSpec((size, quarter), lambda i: (0, 0)),
            pl.BlockSpec((rows // 4, cols), lambda i: (i, 0)),
        ],
        out_specs=(
            pl.BlockSpec((step, quarter), lambda i: (i, 0)),
            pl.BlockSpec((step, quarter), lambda i: (i, 0)),
            pl.BlockSpec((rows // 4, cols), lambda i: (i, 0)),
        ),
        compiler_params=pltpu.CompilerParams(vmem_limit_bytes=32 * 2**20),
        name="grams",
    )(blocks.reshape(size, quarter), weight_grad)
    return (
        input_grad,
        weight_grad,
        left.reshape(1, 1, 1, size, quarter),
        right.reshape(1, 1, 1, quarter, quarter),
    )


def solution(mesh):
    return jax.shard_map(
        on_device,
        mesh=mesh,
        in_specs=(P("col", "row"), P("row", "col"), P("row", "col")),
        out_specs=(
            P("col", "row"),
            P("row", "col"),
            P("row", "col", None, None, None),
            P("row", "col", None, None, None),
        ),
        check_vma=False,
    )
```

time: 82.4 us -> 75.2 us (0.913)
  the two profiles are of different devices: /device:TPU:21 before, /device:TPU:1 now
where the time goes in v2:
time: 75.2 us; the launch traced here: 75 us
  Pallas kernels  70.3 us (93%)
  local copies, waits for them, and re-layouts  4 us (5%)
    pallas_call x1, Pallas kernels, on_device(): pl.pallas_call(gather_kernel, out_shape=(jax.ShapeDtypeStruct((tokens, fe...  64 us
    pallas_call x1, Pallas kernels, on_device(): pl.pallas_call(gram_kernel, grid=(4,), out_shape=(jax.ShapeDtypeStruct((s...  6.34 us
    unnamed x7, local copies, waits for them, and re-layouts  4 us

profile of v2, /device:TPU:1, one launch (start us, length us, event | category | flops | bytes accessed | tf_op | source)
XLA Modules:
  0.0 75.0 jit_solution(17943245095041108937)
XLA Ops:
  0.6 0.0 copy-start
  0.6 1.6 %copy-done = bf16[256,4096]{1,0:T(8,128)(2,1)S(1)} copy-done((bf16[256,4096]{1,0:T(8,128)(2,1)S(1)}, bf16[256,4096]{1,0:T(8,128)(2,1)}, u32[]{:S(2)}) %copy-start) | copy-done | bytes 2097176
  2.2 0.0 copy-start.1
  2.2 0.9 %copy-done.1 = bf16[32,4096]{1,0:T(8,128)(2,1)S(1)} copy-done((bf16[32,4096]{1,0:T(8,128)(2,1)S(1)}, bf16[32,4096]{1,0:T(8,128)(2,1)}, u32[]{:S(2)}) %copy-start.1) | copy-done | bytes 262168
  3.2 0.0 copy-start.2
  3.2 0.8 %copy-done.2 = bf16[128,256]{1,0:T(8,128)(2,1)S(1)} copy-done((bf16[128,256]{1,0:T(8,128)(2,1)S(1)}, bf16[128,256]{1,0:T(8,128)(2,1)}, u32[]{:S(2)}) %copy-start.2) | copy-done | bytes 65560
  4.0 64.0 %gather_and_grads.1 = (bf16[128,256]{1,0:T(8,128)(2,1)S(1)}, bf16[256,4096]{1,0:T(8,128)(2,1)S(1)}, bf16[4,256,1024]{2,1,0:T(8,128)(2,1)S(1)}) custom-call(bf16[128,256]{1,0:T(8,128)(2,1)S(1)} %copy-done.2, bf16[32,4096]{1,0:T(8,128)(2,1)S(1)} %copy-done.1, bf16[256,4096]{1,0:T(8,128)(2,1)S(1)} %copy-done), custom_call_target="tpu_custom_call" | custom-call | tf_op jit(solution)/shard_map/gather_and_grads/pallas_call | solution.py:389
  68.0 6.3 %grams.1 = (f32[1024,1024]{1,0:T(8,128)}, f32[1024,1024]{1,0:T(8,128)}, bf16[256,4096]{1,0:T(8,128)(2,1)}) custom-call(bf16[1024,1024]{1,0:T(8,128)(2,1)S(1)} %bitcast.3, bf16[256,4096]{1,0:T(8,128)(2,1)S(1)} %get-tuple-element.12.wg_in), custom_call_target="tpu_custom_call" | custom-call | tf_op jit(solution)/shard_map/grams/pallas_call | solution.py:421
  74.3 0.6 copy.8
Async XLA Ops:
  0.6 1.6 %copy-start = (bf16[256,4096]{1,0:T(8,128)(2,1)S(1)}, bf16[256,4096]{1,0:T(8,128)(2,1)}, u32[]{:S(2)}) copy-start(bf16[256,4096]{1,0:T(8,128)(2,1)} %w_ref.1) | copy-start | bytes 6291460
  2.2 0.9 %copy-start.1 = (bf16[32,4096]{1,0:T(8,128)(2,1)S(1)}, bf16[32,4096]{1,0:T(8,128)(2,1)}, u32[]{:S(2)}) copy-start(bf16[32,4096]{1,0:T(8,128)(2,1)} %og_ref.1) | copy-start | bytes 786436
  3.2 0.8 %copy-start.2 = (bf16[128,256]{1,0:T(8,128)(2,1)S(1)}, bf16[128,256]{1,0:T(8,128)(2,1)}, u32[]{:S(2)}) copy-start(bf16[128,256]{1,0:T(8,128)(2,1)} %acts_ref.1) | copy-start | bytes 196612

commit v3 on v2

--- a/solution.py
+++ b/solution.py
@@ -23,7 +23,7 @@
     z, line, core = row // 4, lax.rem(row // 2, 2), lax.rem(row, 2)
     x, side = col // 2, lax.rem(col, 2)
     member = 2 * line + core
-    half = og_ref.shape[1] // 2
+    half = og_ref.shape[0] // 2
     quarter = og_ref.shape[1] // 4
     up = (lax.rem(z + 1, 8) * 4 + member, col)
     down = (lax.rem(z + 7, 8) * 4 + member, col)
@@ -55,7 +55,7 @@
         return lax.rem(z + 8 - distance if way == 0 else z + distance, 8)
 
     def part(ref, which):
-        return ref.at[:, pl.ds(which * half, half)]
+        return ref.at[pl.ds(which * half, half)]
 
     def block(where, of_partner):
         return panel.at[where * 4 + 2 * (1 - line if of_partner else line) + core]
@@ -160,14 +160,10 @@
     def input_grad(pieces):
         pieces = [(where, 1 - line if of_partner else line) for where, of_partner in pieces]
 
-        def add(k, total):
-            columns = pl.ds(pl.multiple_of(k * quarter, quarter), quarter)
-            lhs = jnp.concatenate([chunk(*piece, columns) for piece in pieces], axis=0)
-            return total + lax.dot_general(
-                lhs, w_v[:, columns], (((1,), (1,)), ((), ())), preferred_element_type=F32
-            )
-
-        total = lax.fori_loop(0, 4, add, jnp.zeros((64 * len(pieces), w_v.shape[0]), F32))
+        lhs = jnp.concatenate([chunk(*piece, pl.ds(0, 4 * quarter)) for piece in pieces], axis=0)
+        total = lax.dot_general(
+            lhs, w_v[...], (((1,), (1,)), ((), ())), preferred_element_type=F32
+        )
         for i, (where, of_line) in enumerate(pieces):
             value = total[i * 64:(i + 1) * 64]
             same = lax.rem(where, 2) == side
@@ -198,7 +194,7 @@
             )
 
         def own(t, carry):
-            columns = pl.ds(pl.multiple_of(t * 512, 512), 512)
+            columns = pl.ds(pl.multiple_of(t * quarter, quarter), quarter)
             out = jnp.dot(lhs_of(core, line), rhs_of(columns), preferred_element_type=F32)
             if not first:
                 out = out + wacc[:, columns]
@@ -208,24 +204,23 @@
                 wacc[:, columns] = out
             return carry
 
-        lax.fori_loop(0, 8, own, 0)
+        lax.fori_loop(0, 4, own, 0)
 
         def others(t, carry):
-            which = lax.rem(member + 1 + t // 2, 4)
-            columns = pl.ds(pl.multiple_of(member * quarter + lax.rem(t, 2) * 512, 512), 512)
-            place = pl.ds(pl.multiple_of(lax.rem(t, 2) * 512, 512), 512)
+            which = lax.rem(member + 1 + t, 4)
+            columns = pl.ds(pl.multiple_of(member * quarter, quarter), quarter)
             out = jnp.dot(
                 lhs_of(lax.rem(which, 2), which // 2), rhs_of(columns), preferred_element_type=F32
             )
             if not first:
-                out = out + gacc[which, :, place]
+                out = out + gacc[which]
             if last:
-                g_ref[which, :, place] = out.astype(BF16)
+                g_ref[which] = out.astype(BF16)
             else:
-                gacc[which, :, place] = out
+                gacc[which] = out
             return carry
 
-        lax.fori_loop(0, 6, others, 0)
+        lax.fori_loop(0, 3, others, 0)
 
     def pair(step):
         return [plane(step, 0), plane(step, 1)]
@@ -271,9 +266,6 @@
     input_grad([(where, False) for where in pair(1)])
     from_y_near(1)
     from_z(False, 3, 1)
-    for step in range(1, 4):
-        act_x_wait(step)
-        act_m(lax.rem(x + 4 - step, 4), core).start()
     for where in pair(2):
         from_mate(where, False)
     input_grad([(where, False) for where in pair(2)])
@@ -284,14 +276,17 @@
     for where in pair(1):
         from_mate(where, True)
     input_grad([(where, True) for where in pair(1)])
+    for step in range(1, 4):
+        act_x_wait(step)
+        act_m(lax.rem(x + 4 - step, 4), core).start()
     from_z(True, 2, 0)
     for where in pair(3):
         from_mate(where, False)
     input_grad([(where, False) for where in pair(3)])
     for where in range(4):
         act_m(where, 1 - core).wait_recv()
+    weight_grad([z] + pair(1), first=True)
     from_z(True, 2, 1)
-    weight_grad(pair(1), first=True)
     for which in range(2):
         ywait(3, which)
         hand(plane(4, 0), True, which)
@@ -302,8 +297,7 @@
     from_mate(plane(4, 0), True)
     input_grad([(plane(4, 0), False), (plane(4, 0), True)])
     from_z(True, 3, 0)
-    weight_grad(pair(2))
-    weight_grad([z, plane(4, 0)])
+    weight_grad(pair(2) + [plane(4, 0)])
     from_z(True, 3, 1)
     for where in pair(3):
         from_mate(where, True)
@@ -383,7 +377,7 @@
     tokens, feats = activations.shape
     rows, cols = weight.shape
     vmem = pl.BlockSpec(memory_space=pltpu.VMEM)
-    anywhere = pl.BlockSpec(memory_space=pltpu.HBM)
+    anywhere = pl.BlockSpec(memory_space=pl.ANY)
     dma = pltpu.SemaphoreType.DMA
     quarter = cols // 4
     input_grad, weight_grad, blocks = pl.pallas_call(
@@ -414,7 +408,7 @@
             collective_id=0, has_side_effects=True, vmem_limit_bytes=44 * 2**20
         ),
         name="gather_and_grads",
-    )(activations, out_grad, weight)
+    )(*[pltpu.with_memory_space_constraint(a, pltpu.HBM) for a in (activations, out_grad, weight)])
 
     size = 4 * rows
     step = size // 4

time: 75.2 us -> 67.6 us (0.90)
  Pallas kernels: 70.3 us -> 66.2 us
  local copies, waits for them, and re-layouts: 4 us -> 0.63 us
    pallas_call x1, Pallas kernels: 64 us -> 59.9 us  [on_device(): pl.pallas_call(gather_kernel, out_shape=(jax.ShapeDtypeStruct((tokens, fe...]
    unnamed x7 -> x1, local copies, waits for them, and re-layouts: 4 us -> 0.63 us
where the time goes in v3:
time: 67.6 us; the launch traced here: 67.5 us
  Pallas kernels  66.2 us (98%)
    pallas_call x1, Pallas kernels, on_device(): pl.pallas_call(gather_kernel, out_shape=(jax.ShapeDtypeStruct((tokens, fe...  59.9 us
    pallas_call x1, Pallas kernels, on_device(): pl.pallas_call(gram_kernel, grid=(4,), out_shape=(jax.ShapeDtypeStruct((s...  6.33 us

profile of v3, /device:TPU:1, one launch (start us, length us, event | category | flops | bytes accessed | tf_op | source)
XLA Modules:
  0.0 67.5 jit_solution(8963669610770009483)
XLA Ops:
  0.6 59.9 %gather_and_grads.1 = (bf16[128,256]{1,0:T(8,128)(2,1)S(1)}, bf16[256,4096]{1,0:T(8,128)(2,1)S(1)}, bf16[4,256,1024]{2,1,0:T(8,128)(2,1)S(1)}) custom-call(bf16[128,256]{1,0:T(8,128)(2,1)} %acts_ref.1, bf16[32,4096]{1,0:T(8,128)(2,1)} %og_ref.1, bf16[256,4096]{1,0:T(8,128)(2,1)} %w_ref.1), custom_call_target="tpu_custom_call" | custom-call | tf_op jit(solution)/shard_map/gather_and_grads/pallas_call | solution.py:383
  60.6 6.3 %grams.1 = (f32[1024,1024]{1,0:T(8,128)}, f32[1024,1024]{1,0:T(8,128)}, bf16[256,4096]{1,0:T(8,128)(2,1)}) custom-call(bf16[1024,1024]{1,0:T(8,128)(2,1)S(1)} %bitcast.3, bf16[256,4096]{1,0:T(8,128)(2,1)S(1)} %get-tuple-element.12.wg_in), custom_call_target="tpu_custom_call" | custom-call | tf_op jit(solution)/shard_map/grams/pallas_call | solution.py:415
  66.9 0.6 copy.8

commit v4 on v3

--- a/solution.py
+++ b/solution.py
@@ -15,7 +15,7 @@
 def gather_kernel(
     acts_ref, og_ref, w_ref,
     ig_ref, wg_ref, g_ref,
-    panel, w_v, acts_v, acts, wacc, gacc, wide, wide_in, slim, slim_in,
+    panel, w_v, acts_v, acts, wide, wide_in, slim, slim_in,
     local_sem, zsend, zrecv, ysend, yrecv, msend, mrecv,
     aysend, ayrecv, axsend, axrecv, amsend, amrecv, rsend, rrecv,
 ):
@@ -181,7 +181,7 @@
                 slim[where, of_line] = value.astype(BF16)
                 slim_send(where, of_line).start()
 
-    def weight_grad(planes, first=False, last=False):
+    def weight_grad(planes):
         def lhs_of(of_core, of_line):
             return jnp.concatenate(
                 [acts[of_core, where // 2, 2 * lax.rem(where, 2) + of_line] for where in planes], axis=1
@@ -196,12 +196,7 @@
         def own(t, carry):
             columns = pl.ds(pl.multiple_of(t * quarter, quarter), quarter)
             out = jnp.dot(lhs_of(core, line), rhs_of(columns), preferred_element_type=F32)
-            if not first:
-                out = out + wacc[:, columns]
-            if last:
-                wg_ref[:, columns] = out.astype(BF16)
-            else:
-                wacc[:, columns] = out
+            wg_ref[:, columns] = out.astype(BF16)
             return carry
 
         lax.fori_loop(0, 4, own, 0)
@@ -212,12 +207,7 @@
             out = jnp.dot(
                 lhs_of(lax.rem(which, 2), which // 2), rhs_of(columns), preferred_element_type=F32
             )
-            if not first:
-                out = out + gacc[which]
-            if last:
-                g_ref[which] = out.astype(BF16)
-            else:
-                gacc[which] = out
+            g_ref[which] = out.astype(BF16)
             return carry
 
         lax.fori_loop(0, 3, others, 0)
@@ -283,26 +273,24 @@
     for where in pair(3):
         from_mate(where, False)
     input_grad([(where, False) for where in pair(3)])
+    from_z(True, 2, 1)
+    for where in pair(2):
+        from_mate(where, True)
+    input_grad([(where, True) for where in pair(2)])
     for where in range(4):
         act_m(where, 1 - core).wait_recv()
-    weight_grad([z] + pair(1), first=True)
-    from_z(True, 2, 1)
     for which in range(2):
         ywait(3, which)
         hand(plane(4, 0), True, which)
-    for where in pair(2):
-        from_mate(where, True)
-    input_grad([(where, True) for where in pair(2)])
+    from_z(True, 3, 0)
     from_mate(plane(4, 0), False)
     from_mate(plane(4, 0), True)
     input_grad([(plane(4, 0), False), (plane(4, 0), True)])
-    from_z(True, 3, 0)
-    weight_grad(pair(2) + [plane(4, 0)])
     from_z(True, 3, 1)
     for where in pair(3):
         from_mate(where, True)
     input_grad([(where, True) for where in pair(3)])
-    weight_grad(pair(3), last=True)
+    weight_grad([z] + pair(1) + pair(2) + pair(3) + [plane(4, 0)])
     g_ref[member] = wg_ref[:, pl.ds(pl.multiple_of(member * quarter, quarter), quarter)]
 
     for of_line in range(2):
@@ -359,18 +347,36 @@
     lax.fori_loop(0, 4, drain_sums, 0)
 
 
-def gram_kernel(g_ref, wg_in, left_ref, right_ref, wg_out):
-    i = pl.program_id(0)
-    size = left_ref.shape[0]
-    rows = pl.ds(pl.multiple_of(i * size, size), size)
-    wg_out[...] = wg_in[...]
-    scale = 1.0 / g_ref.shape[0]
-    left_ref[...] = scale * lax.dot_general(
-        g_ref[rows, :], g_ref[...], (((1,), (1,)), ((), ())), preferred_element_type=F32
-    )
-    right_ref[...] = scale * lax.dot_general(
-        g_ref[:, rows], g_ref[...], (((0,), (0,)), ((), ())), preferred_element_type=F32
-    )
+def gram_kernel(g_ref, wg_in, left_ref, right_ref, wg_out, left_v, right_v, sem):
+    size = g_ref.shape[0]
+    step = size // 4
+    scale = 1.0 / size
+    copies = [pltpu.make_async_copy(wg_in, wg_out, sem.at[8])]
+    copies[0].start()
+    for kind, (out_v, out_ref) in enumerate(((left_v, left_ref), (right_v, right_ref))):
+        for i in range(4):
+            low = i * step
+            if kind == 0:
+                out = lax.dot_general(
+                    g_ref[low:low + step, :], g_ref[low:, :], (((1,), (1,)), ((), ())),
+                    preferred_element_type=F32,
+                )
+            else:
+                out = lax.dot_general(
+                    g_ref[:, low:low + step], g_ref[:, low:], (((0,), (0,)), ((), ())),
+                    preferred_element_type=F32,
+                )
+            out = out * scale
+            out_v[low:low + step, low:] = out
+            for j in range(i + 1, 4):
+                block = out[:, (j - i) * step:(j - i + 1) * step]
+                out_v[j * step:(j + 1) * step, low:low + step] = block.T
+            rows = pl.ds(low, step)
+            copy = pltpu.make_async_copy(out_v.at[rows], out_ref.at[rows], sem.at[kind * 4 + i])
+            copy.start()
+            copies.append(copy)
+    for copy in copies:
+        copy.wait()
 
 
 def on_device(activations, out_grad, weight):
@@ -394,8 +400,6 @@
             pltpu.VMEM((rows, cols), BF16),
             pltpu.VMEM((tokens, feats), BF16),
             pltpu.VMEM((2, 4, 4, feats, tokens), BF16),
-            pltpu.VMEM((rows, cols), F32),
-            pltpu.VMEM((4, rows, quarter), F32),
             pltpu.VMEM((8, 2, tokens // 2, feats), F32),
             pltpu.VMEM((8, 2, tokens // 2, feats), F32),
             pltpu.VMEM((8, 2, tokens // 2, feats), BF16),
@@ -411,24 +415,18 @@
     )(*[pltpu.with_memory_space_constraint(a, pltpu.HBM) for a in (activations, out_grad, weight)])
 
     size = 4 * rows
-    step = size // 4
     left, right, weight_grad = pl.pallas_call(
         gram_kernel,
-        grid=(4,),
         out_shape=(
             jax.ShapeDtypeStruct((size, quarter), F32),
             jax.ShapeDtypeStruct((quarter, quarter), F32),
             jax.ShapeDtypeStruct((rows, cols), BF16),
         ),
-        in_specs=[
-            pl.BlockSpec((size, quarter), lambda i: (0, 0)),
-            pl.BlockSpec((rows // 4, cols), lambda i: (i, 0)),
+        in_specs=[vmem, vmem],
+        out_specs=(anywhere, anywhere, anywhere),
+        scratch_shapes=[
+            pltpu.VMEM((size, quarter), F32), pltpu.VMEM((quarter, quarter), F32), dma((9,)),
         ],
-        out_specs=(
-            pl.BlockSpec((step, quarter), lambda i: (i, 0)),
-            pl.BlockSpec((step, quarter), lambda i: (i, 0)),
-            pl.BlockSpec((rows // 4, cols), lambda i: (i, 0)),
-        ),
         compiler_params=pltpu.CompilerParams(vmem_limit_bytes=32 * 2**20),
         name="grams",
     )(blocks.reshape(size, quarter), weight_grad)

time: 67.6 us -> 63.7 us (0.942)
  Pallas kernels: 66.2 us -> 62.4 us
    pallas_call x1, Pallas kernels: 59.9 us -> 57.9 us  [on_device(): pl.pallas_call(gather_kernel, out_shape=(jax.ShapeDtypeStruct((tokens, fe...]
    pallas_call x1, Pallas kernels: 6.33 us -> 4.47 us  [on_device(): pl.pallas_call(gram_kernel, out_shape=(jax.ShapeDtypeStruct((size, quarte...]
where the time goes in v4:
time: 63.7 us; the launch traced here: 63.6 us
  Pallas kernels  62.4 us (98%)
  between operations  0.65 us (1%)
    pallas_call x1, Pallas kernels, on_device(): pl.pallas_call(gather_kernel, out_shape=(jax.ShapeDtypeStruct((tokens, fe...  57.9 us
    pallas_call x1, Pallas kernels, on_device(): pl.pallas_call(gram_kernel, out_shape=(jax.ShapeDtypeStruct((size, quarte...  4.47 us

profile of v4, /device:TPU:1, one launch (start us, length us, event | category | flops | bytes accessed | tf_op | source)
XLA Modules:
  0.0 63.6 jit_solution(6734336486013058666)
XLA Ops:
  0.6 57.9 %gather_and_grads.1 = (bf16[128,256]{1,0:T(8,128)(2,1)S(1)}, bf16[256,4096]{1,0:T(8,128)(2,1)S(1)}, bf16[4,256,1024]{2,1,0:T(8,128)(2,1)S(1)}) custom-call(bf16[128,256]{1,0:T(8,128)(2,1)} %acts_ref.1, bf16[32,4096]{1,0:T(8,128)(2,1)} %og_ref.1, bf16[256,4096]{1,0:T(8,128)(2,1)} %w_ref.1), custom_call_target="tpu_custom_call" | custom-call | tf_op jit(solution)/shard_map/gather_and_grads/pallas_call | solution.py:389
  58.5 4.5 %grams.1 = (f32[1024,1024]{1,0:T(8,128)}, f32[1024,1024]{1,0:T(8,128)}, bf16[256,4096]{1,0:T(8,128)(2,1)}) custom-call(bf16[1024,1024]{1,0:T(8,128)(2,1)S(1)} %bitcast.3, bf16[256,4096]{1,0:T(8,128)(2,1)S(1)} %get-tuple-element.12.wg_in), custom_call_target="tpu_custom_call" | custom-call | tf_op jit(solution)/shard_map/grams/pallas_call | solution.py:418
  63.0 0.6 copy.8

commit v5 on v4

--- a/solution.py
+++ b/solution.py
@@ -247,15 +247,15 @@
     w_copy.wait()
     from_mate(z, False)
     from_z(False, 2, 1)
-    from_y_near(0)
     from_mate(z, True)
     input_grad([(z, False), (z, True)])
     from_z(False, 3, 0)
+    from_y_near(0)
     for where in pair(1):
         from_mate(where, False)
     input_grad([(where, False) for where in pair(1)])
+    from_z(False, 3, 1)
     from_y_near(1)
-    from_z(False, 3, 1)
     for where in pair(2):
         from_mate(where, False)
     input_grad([(where, False) for where in pair(2)])
@@ -272,7 +272,8 @@
     from_z(True, 2, 0)
     for where in pair(3):
         from_mate(where, False)
-    input_grad([(where, False) for where in pair(3)])
+    from_mate(plane(4, 0), False)
+    input_grad([(where, False) for where in pair(3)] + [(plane(4, 0), False)])
     from_z(True, 2, 1)
     for where in pair(2):
         from_mate(where, True)
@@ -283,13 +284,11 @@
         ywait(3, which)
         hand(plane(4, 0), True, which)
     from_z(True, 3, 0)
-    from_mate(plane(4, 0), False)
-    from_mate(plane(4, 0), True)
-    input_grad([(plane(4, 0), False), (plane(4, 0), True)])
     from_z(True, 3, 1)
     for where in pair(3):
         from_mate(where, True)
-    input_grad([(where, True) for where in pair(3)])
+    from_mate(plane(4, 0), True)
+    input_grad([(where, True) for where in pair(3)] + [(plane(4, 0), True)])
     weight_grad([z] + pair(1) + pair(2) + pair(3) + [plane(4, 0)])
     g_ref[member] = wg_ref[:, pl.ds(pl.multiple_of(member * quarter, quarter), quarter)]
 
@@ -347,12 +346,18 @@
     lax.fori_loop(0, 4, drain_sums, 0)
 
 
-def gram_kernel(g_ref, wg_in, left_ref, right_ref, wg_out, left_v, right_v, sem):
+def gram_kernel(
+    g_ref, wg_in, ig_in, left_ref, right_ref, wg_out, ig_out, left_v, right_v, sem
+):
     size = g_ref.shape[0]
     step = size // 4
     scale = 1.0 / size
-    copies = [pltpu.make_async_copy(wg_in, wg_out, sem.at[8])]
-    copies[0].start()
+    copies = [
+        pltpu.make_async_copy(wg_in, wg_out, sem.at[8]),
+        pltpu.make_async_copy(ig_in, ig_out, sem.at[9]),
+    ]
+    for copy in copies:
+        copy.start()
     for kind, (out_v, out_ref) in enumerate(((left_v, left_ref), (right_v, right_ref))):
         for i in range(4):
             low = i * step
@@ -415,21 +420,22 @@
     )(*[pltpu.with_memory_space_constraint(a, pltpu.HBM) for a in (activations, out_grad, weight)])
 
     size = 4 * rows
-    left, right, weight_grad = pl.pallas_call(
+    left, right, weight_grad, input_grad = pl.pallas_call(
         gram_kernel,
         out_shape=(
             jax.ShapeDtypeStruct((size, quarter), F32),
             jax.ShapeDtypeStruct((quarter, quarter), F32),
             jax.ShapeDtypeStruct((rows, cols), BF16),
+            jax.ShapeDtypeStruct((tokens, feats), BF16),
         ),
-        in_specs=[vmem, vmem],
-        out_specs=(anywhere, anywhere, anywhere),
+        in_specs=[vmem, vmem, vmem],
+        out_specs=(anywhere,) * 4,
         scratch_shapes=[
-            pltpu.VMEM((size, quarter), F32), pltpu.VMEM((quarter, quarter), F32), dma((9,)),
+            pltpu.VMEM((size, quarter), F32), pltpu.VMEM((quarter, quarter), F32), dma((10,)),
         ],
         compiler_params=pltpu.CompilerParams(vmem_limit_bytes=32 * 2**20),
         name="grams",
-    )(blocks.reshape(size, quarter), weight_grad)
+    )(blocks.reshape(size, quarter), weight_grad, input_grad)
     return (
         input_grad,
         weight_grad,

time: 63.7 us -> 60.2 us (0.945)
  Pallas kernels: 62.4 us -> 59.5 us
    pallas_call x1, Pallas kernels: 57.9 us -> 55 us  [on_device(): pl.pallas_call(gather_kernel, out_shape=(jax.ShapeDtypeStruct((tokens, fe...]
where the time goes in v5:
time: 60.2 us; the launch traced here: 60.1 us
  Pallas kernels  59.5 us (99%)
  between operations  0.64 us (1%)
    pallas_call x1, Pallas kernels, on_device(): pl.pallas_call(gather_kernel, out_shape=(jax.ShapeDtypeStruct((tokens, fe...  55 us
    pallas_call x1, Pallas kernels, on_device(): pl.pallas_call(gram_kernel, out_shape=(jax.ShapeDtypeStruct((size, quarte...  4.48 us

profile of v5, /device:TPU:1, one launch (start us, length us, event | category | flops | bytes accessed | tf_op | source)
XLA Modules:
  0.0 60.1 jit_solution(2142094052793408289)
XLA Ops:
  0.6 55.0 %gather_and_grads.1 = (bf16[128,256]{1,0:T(8,128)(2,1)S(1)}, bf16[256,4096]{1,0:T(8,128)(2,1)S(1)}, bf16[4,256,1024]{2,1,0:T(8,128)(2,1)S(1)}) custom-call(bf16[128,256]{1,0:T(8,128)(2,1)} %acts_ref.1, bf16[32,4096]{1,0:T(8,128)(2,1)} %og_ref.1, bf16[256,4096]{1,0:T(8,128)(2,1)} %w_ref.1), custom_call_target="tpu_custom_call" | custom-call | tf_op jit(solution)/shard_map/gather_and_grads/pallas_call | solution.py:394
  55.6 4.5 %grams.1 = (f32[1024,1024]{1,0:T(8,128)}, f32[1024,1024]{1,0:T(8,128)}, bf16[256,4096]{1,0:T(8,128)(2,1)}, bf16[128,256]{1,0:T(8,128)(2,1)}) custom-call(bf16[1024,1024]{1,0:T(8,128)(2,1)S(1)} %bitcast.3, bf16[256,4096]{1,0:T(8,128)(2,1)S(1)} %get-tuple-element.12.wg_in, bf16[128,256]{1,0:T(8,128)(2,1)S(1)} %get-tuple-element.13.ig_in), custom_call_target="tpu_custom_call" | custom-call | tf_op jit(solution)/shard_map/grams/pallas_call | solution.py:423

commit v6 on v5

--- a/solution.py
+++ b/solution.py
@@ -266,20 +266,18 @@
     for where in pair(1):
         from_mate(where, True)
     input_grad([(where, True) for where in pair(1)])
-    for step in range(1, 4):
-        act_x_wait(step)
-        act_m(lax.rem(x + 4 - step, 4), core).start()
     from_z(True, 2, 0)
     for where in pair(3):
         from_mate(where, False)
     from_mate(plane(4, 0), False)
     input_grad([(where, False) for where in pair(3)] + [(plane(4, 0), False)])
     from_z(True, 2, 1)
+    for step in range(1, 4):
+        act_x_wait(step)
+        act_m(lax.rem(x + 4 - step, 4), core).start()
     for where in pair(2):
         from_mate(where, True)
     input_grad([(where, True) for where in pair(2)])
-    for where in range(4):
-        act_m(where, 1 - core).wait_recv()
     for which in range(2):
         ywait(3, which)
         hand(plane(4, 0), True, which)
@@ -289,6 +287,8 @@
         from_mate(where, True)
     from_mate(plane(4, 0), True)
     input_grad([(where, True) for where in pair(3)] + [(plane(4, 0), True)])
+    for where in range(4):
+        act_m(where, 1 - core).wait_recv()
     weight_grad([z] + pair(1) + pair(2) + pair(3) + [plane(4, 0)])
     g_ref[member] = wg_ref[:, pl.ds(pl.multiple_of(member * quarter, quarter), quarter)]
 

time: 60.2 us -> 60.2 us (level)
  no operation moved by 1% of the time
where the time goes in v6:
time: 60.2 us; the launch traced here: 60.1 us
  Pallas kernels  59.5 us (99%)
  between operations  0.64 us (1%)
    pallas_call x1, Pallas kernels, on_device(): pl.pallas_call(gather_kernel, out_shape=(jax.ShapeDtypeStruct((tokens, fe...  55 us
    pallas_call x1, Pallas kernels, on_device(): pl.pallas_call(gram_kernel, out_shape=(jax.ShapeDtypeStruct((size, quarte...  4.48 us

profile of v6, /device:TPU:1, one launch (start us, length us, event | category | flops | bytes accessed | tf_op | source)
XLA Modules:
  0.0 60.1 jit_solution(10182330628755790017)
XLA Ops:
  0.6 55.0 %gather_and_grads.1 = (bf16[128,256]{1,0:T(8,128)(2,1)S(1)}, bf16[256,4096]{1,0:T(8,128)(2,1)S(1)}, bf16[4,256,1024]{2,1,0:T(8,128)(2,1)S(1)}) custom-call(bf16[128,256]{1,0:T(8,128)(2,1)} %acts_ref.1, bf16[32,4096]{1,0:T(8,128)(2,1)} %og_ref.1, bf16[256,4096]{1,0:T(8,128)(2,1)} %w_ref.1), custom_call_target="tpu_custom_call" | custom-call | tf_op jit(solution)/shard_map/gather_and_grads/pallas_call | solution.py:394
  55.6 4.5 %grams.1 = (f32[1024,1024]{1,0:T(8,128)}, f32[1024,1024]{1,0:T(8,128)}, bf16[256,4096]{1,0:T(8,128)(2,1)}, bf16[128,256]{1,0:T(8,128)(2,1)}) custom-call(bf16[1024,1024]{1,0:T(8,128)(2,1)S(1)} %bitcast.3, bf16[256,4096]{1,0:T(8,128)(2,1)S(1)} %get-tuple-element.12.wg_in, bf16[128,256]{1,0:T(8,128)(2,1)S(1)} %get-tuple-element.13.ig_in), custom_call_target="tpu_custom_call" | custom-call | tf_op jit(solution)/shard_map/grams/pallas_call | solution.py:423
